TPU v7x, 128 devices: a whole 4x4x4 slice. The times are simulated.
128 devices in a mesh: row: 2 (over core), col: 2 (over x_hi), layer: 32 (over z, y, x_lo).
Axes of the slice: x: 4 (x_hi: 2, x_lo: 2; x = x_hi * 2 + x_lo), y: 4, z: 4, core: 2. Of those that a mesh axis runs over, the one named last changes fastest.
Arguments:
- a_tiles: bfloat16 [2, 2, 32, 64, 128, 128], P('row', 'col', 'layer'), may hold values from -6 to 6
- p_tiles: bfloat16 [2, 2, 32, 16, 128, 128], P('row', 'col', 'layer'), may hold values from -0.015625 to 0.015625
- pair_a: int32 [2, 2, 32, 2, 128, 16], P('row', 'col', 'layer'), may hold values from 0 to 63
- pair_p: int32 [2, 2, 32, 2, 128, 16], P('row', 'col', 'layer'), may hold values from 0 to 31
Outputs:
- c_tiles: bfloat16 [2, 2, 128, 128, 128], P('row', 'col', 'layer')
All inputs are finite; a program needn't handle non-finite values.
Results may differ from a plain program's by a relative error of at most 0.0014.
Values may be sent and summed in bfloat16 or wider, within the bound.
A program may use at most 128 MiB of HBM per device.

v0:
```python
import math

import jax
import jax.numpy as jnp
from jax import lax
from jax.sharding import PartitionSpec as P


def products(source_a, source_p, index_a, index_p):
    slot_count = index_a.shape[0]
    fan_count = index_a.shape[1]
    width = source_a.shape[-1]
    group_size = math.gcd(slot_count, 16)

    def one_group(chosen):
        left = jnp.take(source_a, chosen[0], axis=0)
        right = jnp.take(source_p, chosen[1], axis=0)
        return jnp.einsum("sfij,sfjk->sik", left, right, preferred_element_type=jnp.float32)

    shaped_a = index_a.reshape(slot_count // group_size, group_size, fan_count)
    shaped_p = index_p.reshape(slot_count // group_size, group_size, fan_count)
    results = lax.map(one_group, (shaped_a, shaped_p))
    return results.reshape(slot_count, width, width)


def on_device(a_tiles, p_tiles, pair_a, pair_p):
    local_a = a_tiles[0, 0, 0]
    local_p = p_tiles[0, 0, 0]
    pairs_a = pair_a[0, 0, 0]
    pairs_p = pair_p[0, 0, 0]
    columns = pairs_a.shape[0]
    slots = pairs_a.shape[1]
    per_col = pairs_a.shape[2]
    held = local_a.shape[0]
    gathered_p = lax.all_gather(local_p, "row", axis=0, tiled=True)
    offsets = (jnp.arange(columns, dtype=jnp.int32) * held)[:, None, None]
    glob_a = jnp.transpose(pairs_a + offsets, (1, 0, 2)).reshape(slots, columns * per_col)
    glob_p = jnp.transpose(pairs_p, (1, 0, 2)).reshape(slots, columns * per_col)
    gathered_a = lax.all_gather(local_a, "col", axis=0, tiled=True)
    partial_value = products(gathered_a, gathered_p, glob_a, glob_p)
    merged = lax.psum_scatter(partial_value, "layer", scatter_dimension=0, tiled=True)
    return merged.astype(jnp.bfloat16)[None, None]


def solution(mesh):
    in_specs = (
        P("row", "col", "layer", None, None, None),
        P("row", "col", "layer", None, None, None),
        P("row", "col", "layer", None, None, None),
        P("row", "col", "layer", None, None, None),
    )
    out_specs = P("row", "col", "layer", None, None)
    return jax.shard_map(
        on_device, mesh=mesh, in_specs=in_specs, out_specs=out_specs, check_vma=False
    )
```

profile of v0, /device:TPU:0, one launch (start us, length us, event | category | flops | bytes accessed | tf_op | source)
XLA Modules:
  0.0 655.8 jit_solution(9654542997942818843)
XLA Ops:
  23.2 63.8 %all-gather.5.cloned.1.call-done = bf16[1,1,1,128,128,128]{5,4,2,1,0,3:T(8,128)(2,1)} async-done(((bf16[1,1,1,64,128,128]{5,4,2,1,0,3:T(8,128)(2,1)}), bf16[1,1,1,128,128,128]{5,4,2,1,0,3:T(8,128)(2,1)}) %all-gather.5.cloned.1.call-update) | async-done | bytes 4194320 | tf_op jit(solution)/shard_map/all_gather | solution.py:39
  87.0 363.6 %while.10 = (s32[]{:T(128)}, f32[8,16,128,128]{3,2,1,0:T(8,128)}, s32[8,16,32]{2,1,0:T(8,128)S(1)}, bf16[128,128,128]{2,1,0:T(8,128)(2,1)}, s32[8,16,32]{2,1,0:T...) while((s32[]{:T(128)}, f32[8,16,128,128]{3,2,1,0:T(8,128)}, s32[8,16,32]{2,1,0:T(8,128)S(1)}, ...), condition=%wide.region_1.2_spmd, body=%wide.region_0.1_spmd.sunk | while | flops 2164272128 | bytes 101751376 | solution.py:22
  87.1 15.1 %gather_fusion = bf16[512,128,128]{2,1,0:T(8,128)(2,1)} fusion(bf16[32,128,128]{2,1,0:T(8,128)(2,1)} %get-tuple-element.130, s32[1024]{0:T(1024)S(1)} %pad_clamp_fusion.4), kind=kCustom, calls=%fused_computation.1.clone.1 | custom fusion | bytes 33556480 | tf_op jit(solution)/shard_map/while/body/eval_jaxpr/jit(_take)/gather | solution.py:17
  102.3 16.1 %gather_fusion.1 = bf16[512,128,128]{2,1,0:T(8,128)(2,1)} fusion(bf16[128,128,128]{2,1,0:T(8,128)(2,1)} %get-tuple-element.128, s32[1024]{0:T(1024)S(1)} %pad_clamp_fusion.5), kind=kCustom, calls=%fused_computation.clone.1 | custom fusion | bytes 33556480 | tf_op jit(solution)/shard_map/while/body/eval_jaxpr/jit(_take)/gather | solution.py:16
  118.4 14.1 %fusion.23 = f32[8,16,128,128]{3,2,1,0:T(8,128)} fusion(f32[8,16,128,128]{3,2,1,0:T(8,128)} %get-tuple-element.119, s32[]{:T(128)} %get-tuple-element.118, bf16[16,32,128,128]{3,2,1,0:T(8,128)(2,1)} %bitcast.56, pred[16,32]{1,0:T(8,128)(4,1)S(1)} %get-tuple-element.108, bf16[16,32,128,128]{3,2,1,0:T(8,128)(2,1)} %bitcast.57, ...), kind=kOutput, calls=%fused_computation.9.clone.1 | convolution fusion | flops 2164260864 | bytes 34604544 | tf_op jit(solution)/shard_map/while/body/eval_jaxpr/sfij,sfjk->sik/dot_general | solution.py:18
  132.6 15.1 %gather_fusion = bf16[512,128,128]{2,1,0:T(8,128)(2,1)} fusion(bf16[32,128,128]{2,1,0:T(8,128)(2,1)} %get-tuple-element.130, s32[1024]{0:T(1024)S(1)} %pad_clamp_fusion.4), kind=kCustom, calls=%fused_computation.1.clone.1 | custom fusion | bytes 33556480 | tf_op jit(solution)/shard_map/while/body/eval_jaxpr/jit(_take)/gather | solution.py:17
  147.8 16.1 %gather_fusion.1 = bf16[512,128,128]{2,1,0:T(8,128)(2,1)} fusion(bf16[128,128,128]{2,1,0:T(8,128)(2,1)} %get-tuple-element.128, s32[1024]{0:T(1024)S(1)} %pad_clamp_fusion.5), kind=kCustom, calls=%fused_computation.clone.1 | custom fusion | bytes 33556480 | tf_op jit(solution)/shard_map/while/body/eval_jaxpr/jit(_take)/gather | solution.py:16
  163.9 14.0 %fusion.23 = f32[8,16,128,128]{3,2,1,0:T(8,128)} fusion(f32[8,16,128,128]{3,2,1,0:T(8,128)} %get-tuple-element.119, s32[]{:T(128)} %get-tuple-element.118, bf16[16,32,128,128]{3,2,1,0:T(8,128)(2,1)} %bitcast.56, pred[16,32]{1,0:T(8,128)(4,1)S(1)} %get-tuple-element.108, bf16[16,32,128,128]{3,2,1,0:T(8,128)(2,1)} %bitcast.57, ...), kind=kOutput, calls=%fused_computation.9.clone.1 | convolution fusion | flops 2164260864 | bytes 34604544 | tf_op jit(solution)/shard_map/while/body/eval_jaxpr/sfij,sfjk->sik/dot_general | solution.py:18
  178.0 15.1 %gather_fusion = bf16[512,128,128]{2,1,0:T(8,128)(2,1)} fusion(bf16[32,128,128]{2,1,0:T(8,128)(2,1)} %get-tuple-element.130, s32[1024]{0:T(1024)S(1)} %pad_clamp_fusion.4), kind=kCustom, calls=%fused_computation.1.clone.1 | custom fusion | bytes 33556480 | tf_op jit(solution)/shard_map/while/body/eval_jaxpr/jit(_take)/gather | solution.py:17
  193.2 16.1 %gather_fusion.1 = bf16[512,128,128]{2,1,0:T(8,128)(2,1)} fusion(bf16[128,128,128]{2,1,0:T(8,128)(2,1)} %get-tuple-element.128, s32[1024]{0:T(1024)S(1)} %pad_clamp_fusion.5), kind=kCustom, calls=%fused_computation.clone.1 | custom fusion | bytes 33556480 | tf_op jit(solution)/shard_map/while/body/eval_jaxpr/jit(_take)/gather | solution.py:16
  223.5 15.1 %gather_fusion = bf16[512,128,128]{2,1,0:T(8,128)(2,1)} fusion(bf16[32,128,128]{2,1,0:T(8,128)(2,1)} %get-tuple-element.130, s32[1024]{0:T(1024)S(1)} %pad_clamp_fusion.4), kind=kCustom, calls=%fused_computation.1.clone.1 | custom fusion | bytes 33556480 | tf_op jit(solution)/shard_map/while/body/eval_jaxpr/jit(_take)/gather | solution.py:17
  238.7 16.1 %gather_fusion.1 = bf16[512,128,128]{2,1,0:T(8,128)(2,1)} fusion(bf16[128,128,128]{2,1,0:T(8,128)(2,1)} %get-tuple-element.128, s32[1024]{0:T(1024)S(1)} %pad_clamp_fusion.5), kind=kCustom, calls=%fused_computation.clone.1 | custom fusion | bytes 33556480 | tf_op jit(solution)/shard_map/while/body/eval_jaxpr/jit(_take)/gather | solution.py:16
  254.8 14.1 %fusion.23 = f32[8,16,128,128]{3,2,1,0:T(8,128)} fusion(f32[8,16,128,128]{3,2,1,0:T(8,128)} %get-tuple-element.119, s32[]{:T(128)} %get-tuple-element.118, bf16[16,32,128,128]{3,2,1,0:T(8,128)(2,1)} %bitcast.56, pred[16,32]{1,0:T(8,128)(4,1)S(1)} %get-tuple-element.108, bf16[16,32,128,128]{3,2,1,0:T(8,128)(2,1)} %bitcast.57, ...), kind=kOutput, calls=%fused_computation.9.clone.1 | convolution fusion | flops 2164260864 | bytes 34604544 | tf_op jit(solution)/shard_map/while/body/eval_jaxpr/sfij,sfjk->sik/dot_general | solution.py:18
  268.9 15.1 %gather_fusion = bf16[512,128,128]{2,1,0:T(8,128)(2,1)} fusion(bf16[32,128,128]{2,1,0:T(8,128)(2,1)} %get-tuple-element.130, s32[1024]{0:T(1024)S(1)} %pad_clamp_fusion.4), kind=kCustom, calls=%fused_computation.1.clone.1 | custom fusion | bytes 33556480 | tf_op jit(solution)/shard_map/while/body/eval_jaxpr/jit(_take)/gather | solution.py:17
  284.1 16.1 %gather_fusion.1 = bf16[512,128,128]{2,1,0:T(8,128)(2,1)} fusion(bf16[128,128,128]{2,1,0:T(8,128)(2,1)} %get-tuple-element.128, s32[1024]{0:T(1024)S(1)} %pad_clamp_fusion.5), kind=kCustom, calls=%fused_computation.clone.1 | custom fusion | bytes 33556480 | tf_op jit(solution)/shard_map/while/body/eval_jaxpr/jit(_take)/gather | solution.py:16
  300.3 14.1 %fusion.23 = f32[8,16,128,128]{3,2,1,0:T(8,128)} fusion(f32[8,16,128,128]{3,2,1,0:T(8,128)} %get-tuple-element.119, s32[]{:T(128)} %get-tuple-element.118, bf16[16,32,128,128]{3,2,1,0:T(8,128)(2,1)} %bitcast.56, pred[16,32]{1,0:T(8,128)(4,1)S(1)} %get-tuple-element.108, bf16[16,32,128,128]{3,2,1,0:T(8,128)(2,1)} %bitcast.57, ...), kind=kOutput, calls=%fused_computation.9.clone.1 | convolution fusion | flops 2164260864 | bytes 34604544 | tf_op jit(solution)/shard_map/while/body/eval_jaxpr/sfij,sfjk->sik/dot_general | solution.py:18
  314.4 15.1 %gather_fusion = bf16[512,128,128]{2,1,0:T(8,128)(2,1)} fusion(bf16[32,128,128]{2,1,0:T(8,128)(2,1)} %get-tuple-element.130, s32[1024]{0:T(1024)S(1)} %pad_clamp_fusion.4), kind=kCustom, calls=%fused_computation.1.clone.1 | custom fusion | bytes 33556480 | tf_op jit(solution)/shard_map/while/body/eval_jaxpr/jit(_take)/gather | solution.py:17
  329.6 16.1 %gather_fusion.1 = bf16[512,128,128]{2,1,0:T(8,128)(2,1)} fusion(bf16[128,128,128]{2,1,0:T(8,128)(2,1)} %get-tuple-element.128, s32[1024]{0:T(1024)S(1)} %pad_clamp_fusion.5), kind=kCustom, calls=%fused_computation.clone.1 | custom fusion | bytes 33556480 | tf_op jit(solution)/shard_map/while/body/eval_jaxpr/jit(_take)/gather | solution.py:16
  359.8 15.1 %gather_fusion = bf16[512,128,128]{2,1,0:T(8,128)(2,1)} fusion(bf16[32,128,128]{2,1,0:T(8,128)(2,1)} %get-tuple-element.130, s32[1024]{0:T(1024)S(1)} %pad_clamp_fusion.4), kind=kCustom, calls=%fused_computation.1.clone.1 | custom fusion | bytes 33556480 | tf_op jit(solution)/shard_map/while/body/eval_jaxpr/jit(_take)/gather | solution.py:17
  375.1 16.1 %gather_fusion.1 = bf16[512,128,128]{2,1,0:T(8,128)(2,1)} fusion(bf16[128,128,128]{2,1,0:T(8,128)(2,1)} %get-tuple-element.128, s32[1024]{0:T(1024)S(1)} %pad_clamp_fusion.5), kind=kCustom, calls=%fused_computation.clone.1 | custom fusion | bytes 33556480 | tf_op jit(solution)/shard_map/while/body/eval_jaxpr/jit(_take)/gather | solution.py:16
  405.3 15.1 %gather_fusion = bf16[512,128,128]{2,1,0:T(8,128)(2,1)} fusion(bf16[32,128,128]{2,1,0:T(8,128)(2,1)} %get-tuple-element.130, s32[1024]{0:T(1024)S(1)} %pad_clamp_fusion.4), kind=kCustom, calls=%fused_computation.1.clone.1 | custom fusion | bytes 33556480 | tf_op jit(solution)/shard_map/while/body/eval_jaxpr/jit(_take)/gather | solution.py:17
  420.5 16.1 %gather_fusion.1 = bf16[512,128,128]{2,1,0:T(8,128)(2,1)} fusion(bf16[128,128,128]{2,1,0:T(8,128)(2,1)} %get-tuple-element.128, s32[1024]{0:T(1024)S(1)} %pad_clamp_fusion.5), kind=kCustom, calls=%fused_computation.clone.1 | custom fusion | bytes 33556480 | tf_op jit(solution)/shard_map/while/body/eval_jaxpr/jit(_take)/gather | solution.py:16
  436.6 14.1 %fusion.23 = f32[8,16,128,128]{3,2,1,0:T(8,128)} fusion(f32[8,16,128,128]{3,2,1,0:T(8,128)} %get-tuple-element.119, s32[]{:T(128)} %get-tuple-element.118, bf16[16,32,128,128]{3,2,1,0:T(8,128)(2,1)} %bitcast.56, pred[16,32]{1,0:T(8,128)(4,1)S(1)} %get-tuple-element.108, bf16[16,32,128,128]{3,2,1,0:T(8,128)(2,1)} %bitcast.57, ...), kind=kOutput, calls=%fused_computation.9.clone.1 | convolution fusion | flops 2164260864 | bytes 34604544 | tf_op jit(solution)/shard_map/while/body/eval_jaxpr/sfij,sfjk->sik/dot_general | solution.py:18
  450.7 197.0 %reduce-scatter.2.cloned.1.call-done = f32[4,128,128]{2,1,0:T(8,128)} async-done(((f32[128,128,128]{2,1,0:T(8,128)}), f32[4,128,128]{2,1,0:T(8,128)}) %reduce-scatter.2.cloned.1.call-update) | async-done | bytes 262160 | tf_op jit(solution)/shard_map/reduce_scatter | solution.py:41
  (66 shorter events, 61.8 us)
Async XLA Ops:
  6.5 16.7 %all-gather.7.cloned.1.call-start = ((), (), s32[]{:S(2)}) async-start(), calls=%async_computation.3 | async-start | bytes 1572864 | tf_op jit(solution)/shard_map/all_gather | solution.py:35
  7.3 79.8 %all-gather.5.cloned.1.call-start = ((), (), s32[]{:S(2)}) async-start(), calls=%async_computation.2 | async-start | bytes 6291456 | tf_op jit(solution)/shard_map/all_gather | solution.py:39
  8.0 639.6 %reduce-scatter.2.cloned.1.call-start = ((), (), s32[]{:S(2)}) async-start(), calls=%async_computation.1 | async-start | bytes 8650752 | tf_op jit(solution)/shard_map/reduce_scatter | solution.py:41
Sparse Core Ops, SparseCore 0:
  9.0 14.1 all-gather.6
  24.9 62.1 all-gather.4
  450.8 196.7 reduce-scatter.1
where the time goes:
time: 657 us; the launch traced here: 656 us
  waiting for transfers between devices  275 us (42%)
  local copies, waits for them, and re-layouts  252 us (38%)
  matrix products  112 us (17%)
  between operations  13.1 us (2%)
    reduce_scatter x1, waiting for transfers between devices, on_device(): lax.psum_scatter(partial_value, 'layer', scatter_dimension=0, tiled=True)  197 us
    gather x8, local copies, waits for them, and re-layouts, one_group(): left = jnp.take(source_a, chosen[0], axis=0)  129 us
    gather x8, local copies, waits for them, and re-layouts, one_group(): right = jnp.take(source_p, chosen[1], axis=0)  121 us
    dot_general x8, matrix products, one_group(): jnp.einsum('sfij,sfjk->sik', left, right, preferred_element_type=jnp.floa...  112 us
    all_gather x1, waiting for transfers between devices, on_device(): gathered_a = lax.all_gather(local_a, 'col', axis=0, tiled=True)  63.8 us
    all_gather x1, waiting for transfers between devices, on_device(): gathered_p = lax.all_gather(local_p, 'row', axis=0, tiled=True)  13.2 us
  transfers between devices with their start and end apart: 3, of which 3 were waited for; matrix products, arithmetic and copies ran while one was open for 0% of the time, Pallas kernels for 0%

commit v1 on v0

v1 whole, which is shorter than its diff:
```python
import jax
import jax.numpy as jnp
from jax import lax
from jax.experimental import pallas as pl
from jax.experimental.pallas import tpu as pltpu
from jax.sharding import PartitionSpec as P

TB = 128
FPC = 16
STEPS = 128.0
TOP = 32000.0
TINY = 2.0**-110
HALF = 4 * TB + 16
FULL = 8 * TB + 16
MAGIC = 12582912.0


def encode(tiles, message):
    spots = lax.broadcasted_iota(jnp.int32, (16, TB), 0)
    exponents = jnp.zeros((16, TB), jnp.float32)
    for i, tile in enumerate(tiles):
        top = jnp.maximum(jnp.max(jnp.abs(tile), axis=0, keepdims=True), TINY)
        exponent = jnp.floor(jnp.log2(top) * STEPS) + 2.0
        scaled = tile * (jnp.exp2(exponent * (-1.0 / STEPS)) * TOP)
        whole = ((scaled + MAGIC) - MAGIC).astype(jnp.int32)
        message[i * TB : (i + 1) * TB, :] = whole.astype(jnp.int16)
        exponents = jnp.where(spots == i, exponent, exponents)
    count = len(tiles)
    message[count * TB : count * TB + 16, :] = exponents.astype(jnp.int32).astype(jnp.int16)


def scales(message, count):
    exponents = message[count * TB : count * TB + 16, :].astype(jnp.int32).astype(jnp.float32)
    return jnp.exp2(exponents * (1.0 / STEPS)) * (1.0 / TOP)


def decode(message, scale, i):
    return message[i * TB : (i + 1) * TB, :].astype(jnp.int32).astype(jnp.float32) * scale[i : i + 1, :]


def decode_at(message, scale, i, count):
    spots = lax.broadcasted_iota(jnp.int32, (16, TB), 0)
    row = jnp.sum(jnp.where(spots == i, scale, 0.0), axis=0, keepdims=True)
    rows = pl.ds(pl.multiple_of(i * TB, TB), TB)
    return message[rows, :].astype(jnp.int32).astype(jnp.float32) * row


def kernel(
    pairs, a, p_own, out,
    p_all, p_land, pair_land, pair_mem, own_sum,
    far_out, far_in, near_out, near_in, mid_out, mid_in, last_out, last_in,
    local_sem, p_send, p_recv, pair_send, pair_recv,
    far_send, far_recv, near_send, near_recv, mid_send, mid_recv, last_send, last_recv,
):
    r = lax.axis_index("row")
    q = lax.axis_index("col")
    layer = lax.axis_index("layer")
    z = layer // 8
    y = (layer // 2) % 4
    x_lo = layer % 2

    def device(core, col, grid_zy, low):
        return (core, col, grid_zy * 2 + low)

    zy = z * 4 + y
    sibling = device(1 - r, q, zy, x_lo)
    partner = device(r, 1 - q, zy, x_lo)

    def across(phase, k):
        col = q * (1 - phase) + (1 - q) * phase
        low = x_lo * (1 - k) + (1 - x_lo) * k
        return device(r, col, zy, low)

    def places(o):
        first = z * (1 - o) + y * o
        second = y * (1 - o) + z * o
        return first, second

    def grid_zy(o, first, second):
        return first * (4 - 3 * o) + second * (1 + 3 * o)

    barrier = pltpu.get_barrier_semaphore()
    others = [sibling, partner, across(0, 1), across(1, 1)]
    for shift in (1, 2, 3):
        others.append(device(r, q, ((z + shift) % 4) * 4 + y, x_lo))
        others.append(device(r, q, z * 4 + (y + shift) % 4, x_lo))
    for other in others:
        pl.semaphore_signal(barrier, inc=1, device_id=other, device_id_type=pl.DeviceIdType.MESH)

    mine = pl.ds(r * 16, 16)
    theirs = pl.ds((1 - r) * 16, 16)
    own_copy = pltpu.make_async_copy(p_own, p_all.at[mine], local_sem.at[0])
    pair_copy = pltpu.make_async_copy(pairs.at[q], pair_mem.at[pl.ds(0, 16)], local_sem.at[1])
    own_copy.start()
    pair_copy.start()
    pl.semaphore_wait(barrier, len(others))

    def remote(src, dst, send, recv, to):
        return pltpu.make_async_remote_copy(
            src_ref=src, dst_ref=dst, send_sem=send, recv_sem=recv,
            device_id=to, device_id_type=pl.DeviceIdType.MESH,
        )

    to_sibling = remote(p_own, p_all.at[mine], p_send.at[0], p_recv.at[0], sibling)
    to_sibling.start()
    pairs_over = remote(pairs.at[1 - q], pair_land, pair_send, pair_recv, partner)
    pairs_over.start()
    to_partner = remote(p_own, p_land.at[mine], p_send.at[1], p_recv.at[1], partner)
    to_partner.start()
    forward = remote(p_land.at[mine], p_land.at[mine], p_send.at[2], p_recv.at[2], sibling)
    forward_in = remote(p_land.at[theirs], p_land.at[theirs], p_send.at[2], p_recv.at[2], sibling)
    own_copy.wait()
    pair_copy.wait()
    to_sibling.wait_recv()

    def far(slot, o, d, phase=None):
        first, second = places(o)
        to = device(r, q, grid_zy(o, (first + 1 + 2 * d) % 4, second), x_lo)
        return remote(far_out.at[slot], far_in.at[slot], far_send.at[slot], far_recv.at[slot], to)

    def near(slot, o, d):
        first, second = places(o)
        to = device(r, q, grid_zy(o, (first + 1 + 2 * d) % 4, second), x_lo)
        return remote(near_out.at[slot], near_in.at[slot], near_send.at[slot], near_recv.at[slot], to)

    def flip(second, k):
        high, low = second // 2, second % 2
        k_high, k_low = k // 2, k % 2
        high = high * (1 - k_high) + (1 - high) * k_high
        low = low * (1 - k_low) + (1 - low) * k_low
        return high * 2 + low

    def mid(phase, o, k):
        first, second = places(o)
        slot = (phase * 2 + o) * 3 + k - 1
        to = device(r, q, grid_zy(o, first, flip(second, k)), x_lo)
        return remote(mid_out.at[slot], mid_in.at[slot], mid_send.at[slot], mid_recv.at[slot], to)

    def last(phase, k):
        slot = phase * 2 + k - 1
        return remote(last_out.at[slot], last_in.at[slot], last_send.at[slot], last_recv.at[slot], across(phase, k))

    def product(phase, row, lane):
        total = None
        for g in range(FPC // 2):
            one = pair_mem[phase * 16 + row, lane + 2 * g]
            two = pair_mem[phase * 16 + row, lane + 2 * g + 1]
            left = jnp.concatenate([a[one >> 5], a[two >> 5]], axis=1)
            right = jnp.concatenate([p_all[phase * 32 + (one & 31)], p_all[phase * 32 + (two & 31)]], axis=0)
            part = jnp.dot(left, right, preferred_element_type=jnp.float32)
            total = part if total is None else total + part
        return total

    def far_step(phase):
        @pl.loop(0, 4)
        def _(i):
            o = i % 2
            first, second = places(o)
            h = second // 2
            g = (1 - h) * (1 - i // 2) + h * (i // 2)
            slot = ((phase * 2 + o) * 2 + g) * 2
            sums = [[], []]
            for n in range(2):
                row = grid_zy(o, (first + 2) % 4, g * 2 + n)
                for low in range(2):
                    for j in range(2):
                        sums[j].append(product(phase, row, o * 32 + low * 64 + j * 16))
            for d in range(2):
                encode(sums[d], far_out.at[slot + d])
                far(slot + d, o, d).start()

    def near_step(phase):
        @pl.loop(0, 8)
        def _(i):
            o = i % 2
            d = (i // 2) % 2
            first, second = places(o)
            h = second // 2
            g = (1 - h) * (1 - i // 4) + h * (i // 4)
            slot = ((phase * 2 + o) * 2 + g) * 2 + d
            far(slot, o, d).wait_recv()
            got = far_in.at[slot]
            scale = scales(got, 4)
            sums = []
            for n in range(2):
                row = grid_zy(o, (first + 1 + 2 * d) % 4, g * 2 + n)
                for low in range(2):
                    for j in range(2):
                        place = d * (1 - 2 * j) + j
                        tile = product(phase, row, o * 32 + low * 64 + place * 16)
                        if j == 0:
                            tile = tile + decode(got, scale, n * 2 + low)
                        sums.append(tile)
            encode(sums, near_out.at[slot])
            near(slot, o, d).start()

    def arrived(phase, o, second, low, j):
        slot = ((phase * 2 + o) * 2 + second // 2) * 2
        place = (second % 2) * 4 + low * 2
        plus, minus = near_in.at[slot], near_in.at[slot + 1]
        return decode_at(plus, scales(plus, 8), place + j, 8) + decode_at(minus, scales(minus, 8), place + 1 - j, 8)

    def wait_near(phase, o, g):
        for d in range(2):
            near(((phase * 2 + o) * 2 + g) * 2 + d, o, d).wait_recv()

    def mid_step(phase):
        @pl.loop(0, 3)
        def _(i):
            k = 2 + i - 3 * (i // 2)

            @pl.when(i == 0)
            def _():
                for o in range(2):
                    wait_near(phase, o, 1 - places(o)[1] // 2)

            @pl.when(i == 2)
            def _():
                for o in range(2):
                    wait_near(phase, o, places(o)[1] // 2)

            for o in range(2):
                first, second = places(o)
                there = flip(second, k)
                row = grid_zy(o, first, there)
                sums = []
                for low in range(2):
                    for j in range(2):
                        tile = product(phase, row, o * 32 + low * 64 + j * 16)
                        sums.append(tile + arrived(phase, o, there, low, j))
                encode(sums, mid_out.at[(phase * 2 + o) * 3 + k - 1])
                mid(phase, o, k).start()

    def last_step(phase):
        for o in range(2):
            for k in range(1, 4):
                mid(phase, o, k).wait_recv()
        for k in range(2):
            low = x_lo * (1 - k) + (1 - x_lo) * k
            sums = []
            for o in range(2):
                first, second = places(o)
                messages = [mid_in.at[(phase * 2 + o) * 3 + m] for m in range(3)]
                for j in range(2):
                    tile = product(phase, zy, o * 32 + low * 64 + j * 16)
                    tile = tile + arrived(phase, o, second, low, j)
                    for message in messages:
                        tile = tile + decode_at(message, scales(message, 4), low * 2 + j, 4)
                    sums.append(tile)
            if k == 1:
                encode(sums, last_out.at[phase * 2])
                last(phase, 1).start()
            else:
                @pl.when(phase == 0)
                def _():
                    for i, tile in enumerate(sums):
                        own_sum[i] = tile

                @pl.when(phase == 1)
                def _():
                    encode(sums, last_out.at[1])
                    last(1, 0).start()

    @pl.loop(0, 3)
    def _(step):
        @pl.when(step == 1)
        def _():
            to_partner.wait_recv()
            forward.start()
            pairs_over.wait_recv()
            move = pltpu.make_async_copy(pair_land, pair_mem.at[pl.ds(16, 16)], local_sem.at[1])
            move.start()
            move.wait()
            forward_in.wait_recv()

            @pl.loop(0, 32)
            def _(i):
                p_all[32 + i] = p_land[i]

        @pl.when(step < 2)
        def _():
            far_step(step)

        @pl.when(step > 0)
        def _():
            mid_step(step - 1)

        @pl.when(step < 2)
        def _():
            near_step(step)

        @pl.when(step > 0)
        def _():
            last_step(step - 1)

    for phase, k in ((0, 1), (1, 0), (1, 1)):
        last(phase, k).wait_recv()
    for i in range(4):
        total = own_sum[i]
        for slot in range(3):
            message = last_in.at[slot]
            total = total + decode(message, scales(message, 4), i)
        out[i] = total.astype(out.dtype)

    to_sibling.wait_send()
    to_partner.wait_send()
    forward.wait_send()
    pairs_over.wait_send()

    @pl.loop(0, 16)
    def _(i):
        o, d = (i // 4) % 2, i % 2
        far(i, o, d).wait_send()
        near(i, o, d).wait_send()

    for phase in range(2):
        for o in range(2):
            for k in range(1, 4):
                mid(phase, o, k).wait_send()
    for phase, k in ((0, 1), (1, 0), (1, 1)):
        last(phase, k).wait_send()


def on_device(a_tiles, p_tiles, pair_a, pair_p):
    pairs = (pair_a[0, 0, 0] * 32 + pair_p[0, 0, 0]).reshape(2, 16, TB)
    i16 = jnp.int16
    dma = pltpu.SemaphoreType.DMA
    vmem = pl.BlockSpec(memory_space=pltpu.VMEM)
    anywhere = pl.BlockSpec(memory_space=pl.ANY)
    out = pl.pallas_call(
        kernel,
        out_shape=jax.ShapeDtypeStruct((4, TB, TB), jnp.bfloat16),
        in_specs=[anywhere, vmem, anywhere],
        out_specs=vmem,
        scratch_shapes=[
            pltpu.VMEM((64, TB, TB), jnp.bfloat16),
            pltpu.VMEM((32, TB, TB), jnp.bfloat16),
            pltpu.VMEM((16, TB), jnp.int32),
            pltpu.SMEM((32, TB), jnp.int32),
            pltpu.VMEM((4, TB, TB), jnp.float32),
            pltpu.VMEM((16, HALF, TB), i16),
            pltpu.VMEM((16, HALF, TB), i16),
            pltpu.VMEM((16, FULL, TB), i16),
            pltpu.VMEM((16, FULL, TB), i16),
            pltpu.VMEM((12, HALF, TB), i16),
            pltpu.VMEM((12, HALF, TB), i16),
            pltpu.VMEM((3, HALF, TB), i16),
            pltpu.VMEM((3, HALF, TB), i16),
            dma((2,)), dma((3,)), dma((3,)), dma, dma,
            dma((16,)), dma((16,)), dma((16,)), dma((16,)),
            dma((12,)), dma((12,)), dma((3,)), dma((3,)),
        ],
        compiler_params=pltpu.CompilerParams(
            collective_id=0, has_side_effects=True, vmem_limit_bytes=56 << 20
        ),
        cost_estimate=pl.CostEstimate(flops=2 * 4096 * TB**3, bytes_accessed=4 << 20, transcendentals=0),
    )(pairs, a_tiles[0, 0, 0], p_tiles[0, 0, 0])
    return out[None, None]


def solution(mesh):
    tiles = P("row", "col", "layer", None, None, None)
    return jax.shard_map(
        on_device, mesh=mesh, in_specs=(tiles,) * 4,
        out_specs=P("row", "col", "layer", None, None), check_vma=False,
    )
```

time: 657 us -> 80 us (0.12)
  the two profiles are of different devices: /device:TPU:0 before, /device:TPU:24 now
where the time goes in v1:
time: 80 us; the launch traced here: 79.7 us
  Pallas kernels  76.6 us (96%)
  local copies, waits for them, and re-layouts  2.38 us (3%)
    pallas_call x1, Pallas kernels, on_device(): pl.pallas_call(kernel, out_shape=jax.ShapeDtypeStruct((4, TB, TB), jnp.bf...  76.6 us

profile of v1, /device:TPU:24, one launch (start us, length us, event | category | flops | bytes accessed | tf_op | source)
XLA Modules:
  0.0 79.7 jit_solution(9333961962390548530)
XLA Ops:
  0.0 0.7 multiply_add_fusion
  0.7 0.1 copy.6
  0.8 0.7 add.8.pairs
  1.6 76.6 %shard_map.46 = bf16[4,128,128]{2,1,0:T(8,128)(2,1)} custom-call(s32[2,16,128]{2,1,0:T(8,128)} %add.8.pairs, bf16[64,128,128]{2,1,0:T(8,128)(2,1)} %bitcast.6, bf16[16,128,128]{2,1,0:T(8,128)(2,1)} %bitcast.7), custom_call_target="tpu_custom_call" | custom-call | flops 17179869184 | bytes 4194304 | tf_op jit(solution)/shard_map/pallas_call | solution.py:330
  78.2 1.6 %copy.8 = bf16[1,1,4,128,128]{4,3,2,1,0:T(8,128)(2,1)} copy(bf16[1,1,4,128,128]{4,3,2,1,0:T(8,128)(2,1)} %bitcast.5) | data formatting | bytes 262144

commit v2 on v0

v2 whole, which is shorter than its diff:
```python
import jax
import jax.numpy as jnp
from jax import lax
from jax.experimental import pallas as pl
from jax.experimental.pallas import tpu as pltpu
from jax.sharding import PartitionSpec as P

TB = 128
FPC = 16
STEPS = 128.0
TOP = 32000.0
TINY = 2.0**-110
HALF = 4 * TB + 16
FULL = 8 * TB + 16
PAIR = 2 * TB + 16
MAGIC = 12582912.0

FAR, NEAR, SIDE, MID, HOME, TAKE, SPREAD, OWN = range(8)
ITEMS = (
    (FAR, 1, 0, 0),
    (FAR, 1, 1, 0),
    (FAR, 0, 0, 0),
    (FAR, 0, 1, 0),
    (NEAR, 1, 0, 1),
    (NEAR, 1, 1, 1),
    (NEAR, 1, 1, 0),
    (NEAR, 1, 0, 0),
    (NEAR, 0, 0, 1),
    (TAKE, 0, 0, 0),
    (NEAR, 0, 1, 1),
    (SPREAD, 0, 0, 0),
    (FAR, 2, 0, 0),
    (FAR, 2, 1, 0),
    (FAR, 3, 1, 0),
    (FAR, 3, 0, 0),
    (SIDE, 1, 0, 0),
    (NEAR, 2, 0, 0),
    (NEAR, 2, 1, 0),
    (NEAR, 2, 0, 1),
    (NEAR, 2, 1, 1),
    (SIDE, 1, 1, 0),
    (NEAR, 3, 0, 1),
    (NEAR, 3, 1, 0),
    (NEAR, 3, 0, 0),
    (NEAR, 3, 1, 1),
    (SIDE, 2, 0, 0),
    (NEAR, 0, 0, 0),
    (NEAR, 0, 1, 0),
    (SIDE, 2, 1, 0),
    (MID, 3, 0, 0),
    (MID, 3, 1, 0),
    (HOME, 0, 0, 0),
    (OWN, 0, 0, 0),
    (HOME, 0, 1, 0),
)

def encode(tiles, message):
    spots = lax.broadcasted_iota(jnp.int32, (16, TB), 0)
    exponents = jnp.zeros((16, TB), jnp.float32)
    for i, tile in enumerate(tiles):
        top = jnp.maximum(jnp.max(jnp.abs(tile), axis=0, keepdims=True), TINY)
        exponent = jnp.floor(jnp.log2(top) * STEPS) + 2.0
        scaled = tile * (jnp.exp2(exponent * (-1.0 / STEPS)) * TOP)
        whole = ((scaled + MAGIC) - MAGIC).astype(jnp.int32)
        message[i * TB : (i + 1) * TB, :] = whole.astype(jnp.int16)
        exponents = jnp.where(spots == i, exponent, exponents)
    count = len(tiles)
    message[count * TB : count * TB + 16, :] = exponents.astype(jnp.int32).astype(jnp.int16)


def scales(message, count):
    exponents = message[count * TB : count * TB + 16, :].astype(jnp.int32).astype(jnp.float32)
    return jnp.exp2(exponents * (1.0 / STEPS)) * (1.0 / TOP)


def decode(message, scale, i):
    return message[i * TB : (i + 1) * TB, :].astype(jnp.int32).astype(jnp.float32) * scale[i : i + 1, :]


def decode_at(message, scale, i, count):
    spots = lax.broadcasted_iota(jnp.int32, (16, TB), 0)
    row = jnp.sum(jnp.where(spots == i, scale, 0.0), axis=0, keepdims=True)
    rows = pl.ds(pl.multiple_of(i * TB, TB), TB)
    return message[rows, :].astype(jnp.int32).astype(jnp.float32) * row


def kernel(
    pairs, a, p_own, out,
    p_all, p_land, pair_land, pair_mem, own_sum,
    far_out, far_in, near_out, near_in, side_out, side_in, mid_out, mid_in, last_out, last_in,
    local_sem, p_send, p_recv, pair_send, pair_recv,
    far_send, far_recv, near_send, near_recv, side_send, side_recv, mid_send, mid_recv, last_send, last_recv,
):
    r = lax.axis_index("row")
    q = lax.axis_index("col")
    layer = lax.axis_index("layer")
    z = layer // 8
    y = (layer // 2) % 4
    x_lo = layer % 2
    zy = z * 4 + y

    def turned(bit, by):
        return bit * (1 - by) + (1 - bit) * by

    def flip(place, k):
        return turned(place // 2, k // 2) * 2 + turned(place % 2, k % 2)

    def device(core, col, at, low):
        return (core, col, at * 2 + low)

    def across(k):
        return device(r, turned(q, k // 2), zy, turned(x_lo, k % 2))

    def places(o):
        return z * (1 - o) + y * o, y * (1 - o) + z * o

    def grid_zy(o, first, second):
        return first * (4 - 3 * o) + second * (1 + 3 * o)

    sibling = device(1 - r, q, zy, x_lo)
    partner = across(2)

    barrier = pltpu.get_barrier_semaphore()
    others = [sibling, across(1), partner, across(3)]
    for shift in (1, 2, 3):
        others.append(device(r, q, ((z + shift) % 4) * 4 + y, x_lo))
        others.append(device(r, q, z * 4 + (y + shift) % 4, x_lo))
    for other in others:
        pl.semaphore_signal(barrier, inc=1, device_id=other, device_id_type=pl.DeviceIdType.MESH)

    mine = pl.ds(r * 16, 16)
    theirs = pl.ds((1 - r) * 16, 16)
    own_copy = pltpu.make_async_copy(p_own, p_all.at[mine], local_sem.at[0])
    pair_copy = pltpu.make_async_copy(pairs.at[q], pair_mem.at[pl.ds(0, 16)], local_sem.at[1])
    pair_move = pltpu.make_async_copy(pair_land, pair_mem.at[pl.ds(16, 16)], local_sem.at[2])
    own_copy.start()
    pair_copy.start()
    pl.semaphore_wait(barrier, len(others))

    def remote(src, dst, send, recv, to):
        return pltpu.make_async_remote_copy(
            src_ref=src, dst_ref=dst, send_sem=send, recv_sem=recv,
            device_id=to, device_id_type=pl.DeviceIdType.MESH,
        )

    to_sibling = remote(p_own, p_all.at[mine], p_send.at[0], p_recv.at[0], sibling)
    pairs_over = remote(pairs.at[1 - q], pair_land, pair_send, pair_recv, partner)
    to_partner = remote(p_own, p_land.at[mine], p_send.at[1], p_recv.at[1], partner)
    forward = remote(p_land.at[mine], p_land.at[mine], p_send.at[2], p_recv.at[2], sibling)
    forward_in = remote(p_land.at[theirs], p_land.at[theirs], p_send.at[2], p_recv.at[2], sibling)
    to_sibling.start()
    pairs_over.start()
    to_partner.start()
    own_copy.wait()
    pair_copy.wait()
    to_sibling.wait_recv()

    def along(o, d):
        first, second = places(o)
        return device(r, q, grid_zy(o, (first + 1 + 2 * d) % 4, second), x_lo)

    def far(k, o, d):
        at = (k * 2 + o) * 2 + d
        return remote(far_out.at[at], far_in.at[at], far_send.at[at], far_recv.at[at], along(o, d))

    def near(k, o, d):
        at = (k * 2 + o) * 2 + d
        return remote(near_out.at[at], near_in.at[at], near_send.at[at], near_recv.at[at], along(o, d))

    def side(k, g):
        at = (k - 1) * 2 + g
        return remote(side_out.at[at], side_in.at[at], side_send.at[at], side_recv.at[at], across(k))

    def mid(h, o, kk):
        at = (h * 2 + o) * 3 + kk - 1
        first, second = places(o)
        to = device(r, q, grid_zy(o, first, flip(second, kk)), x_lo)
        return remote(mid_out.at[at], mid_in.at[at], mid_send.at[at], mid_recv.at[at], to)

    last = remote(last_out, last_in, last_send, last_recv, across(3))

    def product(k, at, o, j):
        row = (k // 2) * 16 + at
        lane = turned(x_lo, k % 2) * 64 + o * 32 + j * 16
        first_p = (k // 2) * 32
        total = None
        for g in range(FPC // 2):
            one = pair_mem[row, lane + 2 * g]
            two = pair_mem[row, lane + 2 * g + 1]
            left = jnp.concatenate([a[one >> 5], a[two >> 5]], axis=1)
            right = jnp.concatenate([p_all[first_p + (one & 31)], p_all[first_p + (two & 31)]], axis=0)
            part = jnp.dot(left, right, preferred_element_type=jnp.float32)
            total = part if total is None else total + part
        return total

    def far_item(k, o):
        first, second = places(o)
        sums = [[], []]
        for n in range(4):
            at = grid_zy(o, (first + 2) % 4, n)
            for j in range(2):
                sums[j].append(product(k, at, o, j))
        for d in range(2):
            encode(sums[d], far_out.at[(k * 2 + o) * 2 + d])
            far(k, o, d).start()

    def near_item(k, o, d):
        first, second = places(o)
        far(k, o, d).wait_recv()
        got = far_in.at[(k * 2 + o) * 2 + d]
        scale = scales(got, 4)
        sums = []
        for n in range(4):
            at = grid_zy(o, (first + 1 + 2 * d) % 4, n)
            for j in range(2):
                tile = product(k, at, o, turned(j, d))
                if j == 0:
                    tile = tile + decode(got, scale, n)
                sums.append(tile)
        encode(sums, near_out.at[(k * 2 + o) * 2 + d])
        near(k, o, d).start()

    def mid_sums(k, g, extra):
        @pl.when(g == 0)
        def _():
            for o in range(2):
                for d in range(2):
                    near(k, o, d).wait_recv()

        for m in extra:
            side(m, g).wait_recv()
        sides = [side_in.at[(m - 1) * 2 + g] for m in extra]
        side_scales = [scales(message, 8) for message in sides]
        sums = []
        for o in range(2):
            first, second = places(o)
            plus, minus = near_in.at[(k * 2 + o) * 2], near_in.at[(k * 2 + o) * 2 + 1]
            plus_scale, minus_scale = scales(plus, 8), scales(minus, 8)
            for n in range(2):
                there = flip(second, (2 + n) * (1 - g) + (1 - n) * g)
                at = grid_zy(o, first, there)
                for j in range(2):
                    tile = product(k, at, o, j)
                    tile = tile + decode_at(plus, plus_scale, there * 2 + j, 8)
                    tile = tile + decode_at(minus, minus_scale, there * 2 + 1 - j, 8)
                    for message, scale in zip(sides, side_scales):
                        tile = tile + decode(message, scale, len(sums))
                    sums.append(tile)
        return sums

    def side_item(k, g):
        encode(mid_sums(k, g, ()), side_out.at[(k - 1) * 2 + g])
        side(k, g).start()

    def mid_item(k, h, g, extra):
        sums = mid_sums(k, g, extra)
        for o in range(2):
            kk = 2 - g
            encode(sums[o * 4 : o * 4 + 2], mid_out.at[(h * 2 + o) * 3 + kk - 1])
            mid(h, o, kk).start()

        @pl.when(g == 0)
        def _():
            for o in range(2):
                encode(sums[o * 4 + 2 : o * 4 + 4], mid_out.at[(h * 2 + o) * 3 + 2])
                mid(h, o, 3).start()

        @pl.when(g == 1)
        def _():
            for o in range(2):
                for j in range(2):
                    own_sum[h * 4 + o * 2 + j] = sums[o * 4 + 2 + j]

    def own_item(h):
        sums = []
        for o in range(2):
            messages = []
            for kk in range(1, 4):
                mid(h, o, kk).wait_recv()
                message = mid_in.at[(h * 2 + o) * 3 + kk - 1]
                messages.append((message, scales(message, 2)))
            for j in range(2):
                tile = own_sum[h * 4 + o * 2 + j]
                for message, scale in messages:
                    tile = tile + decode(message, scale, j)
                sums.append(tile)
        if h == 0:
            encode(sums, last_out)
            last.start()
        else:
            for i, tile in enumerate(sums):
                own_sum[4 + i] = tile

    def take_p():
        to_partner.wait_recv()
        forward.start()
        pairs_over.wait_recv()
        pair_move.start()

    def spread_p():
        pair_move.wait()
        forward_in.wait_recv()

        @pl.loop(0, 32)
        def _(i):
            p_all[32 + i] = p_land[i]

    @pl.loop(0, len(ITEMS))
    def _(i):
        code = 0
        for n, item in enumerate(ITEMS):
            code = jnp.where(i == n, ((item[0] * 4 + item[1]) * 2 + item[2]) * 2 + item[3], code)
        kind, k, u, d = code // 16, (code // 4) % 4, (code // 2) % 2, code % 2
        pl.when(kind == FAR)(lambda: far_item(k, u))
        pl.when(kind == NEAR)(lambda: near_item(k, u, d))
        pl.when(kind == SIDE)(lambda: side_item(k, u))
        pl.when(kind == MID)(lambda: mid_item(3, 0, u, ()))
        pl.when(kind == HOME)(lambda: mid_item(0, 1, u, (1, 2)))
        pl.when(kind == TAKE)(take_p)
        pl.when(kind == SPREAD)(spread_p)
        pl.when(kind == OWN)(lambda: own_item(0))
    own_item(1)

    last.wait_recv()
    scale = scales(last_in, 4)
    for i in range(4):
        out[i] = (own_sum[4 + i] + decode(last_in, scale, i)).astype(out.dtype)

    for copy in (to_sibling, to_partner, forward, pairs_over, last):
        copy.wait_send()

    @pl.loop(0, 16)
    def _(i):
        far(i // 4, (i // 2) % 2, i % 2).wait_send()
        near(i // 4, (i // 2) % 2, i % 2).wait_send()

    for k in (1, 2):
        for g in range(2):
            side(k, g).wait_send()
    for h in range(2):
        for o in range(2):
            for kk in range(1, 4):
                mid(h, o, kk).wait_send()


def on_device(a_tiles, p_tiles, pair_a, pair_p):
    pairs = (pair_a[0, 0, 0] * 32 + pair_p[0, 0, 0]).reshape(2, 16, TB)
    i16 = jnp.int16
    dma = pltpu.SemaphoreType.DMA
    vmem = pl.BlockSpec(memory_space=pltpu.VMEM)
    anywhere = pl.BlockSpec(memory_space=pl.ANY)
    out = pl.pallas_call(
        kernel,
        out_shape=jax.ShapeDtypeStruct((4, TB, TB), jnp.bfloat16),
        in_specs=[anywhere, vmem, anywhere],
        out_specs=vmem,
        scratch_shapes=[
            pltpu.VMEM((64, TB, TB), jnp.bfloat16),
            pltpu.VMEM((32, TB, TB), jnp.bfloat16),
            pltpu.VMEM((16, TB), jnp.int32),
            pltpu.SMEM((32, TB), jnp.int32),
            pltpu.VMEM((8, TB, TB), jnp.float32),
            pltpu.VMEM((16, HALF, TB), i16),
            pltpu.VMEM((16, HALF, TB), i16),
            pltpu.VMEM((16, FULL, TB), i16),
            pltpu.VMEM((16, FULL, TB), i16),
            pltpu.VMEM((4, FULL, TB), i16),
            pltpu.VMEM((4, FULL, TB), i16),
            pltpu.VMEM((12, PAIR, TB), i16),
            pltpu.VMEM((12, PAIR, TB), i16),
            pltpu.VMEM((HALF, TB), i16),
            pltpu.VMEM((HALF, TB), i16),
            dma((3,)), dma((3,)), dma((3,)), dma, dma,
            dma((16,)), dma((16,)), dma((16,)), dma((16,)),
            dma((4,)), dma((4,)), dma((12,)), dma((12,)), dma, dma,
        ],
        compiler_params=pltpu.CompilerParams(
            collective_id=0, has_side_effects=True, vmem_limit_bytes=56 << 20
        ),
        cost_estimate=pl.CostEstimate(flops=2 * 4096 * TB**3, bytes_accessed=4 << 20, transcendentals=0),
    )(pairs, a_tiles[0, 0, 0], p_tiles[0, 0, 0])
    return out[None, None]


def solution(mesh):
    tiles = P("row", "col", "layer", None, None, None)
    return jax.shard_map(
        on_device, mesh=mesh, in_specs=(tiles,) * 4,
        out_specs=P("row", "col", "layer", None, None), check_vma=False,
    )
```

time: 657 us -> 73 us (0.11)
  waiting for transfers between devices: 275 us -> 0 us
  local copies, waits for them, and re-layouts: 252 us -> 2.38 us
  matrix products: 112 us -> 0 us
  Pallas kernels: 0 us -> 69.6 us
  between operations: 13.1 us -> 0.01 us
    gather x16 -> x0, local copies, waits for them, and re-layouts: 250 us -> none  [the longest x8 129 us: one_group(): left = jnp.take(source_a, chosen[0], axis=0)]
    reduce_scatter x1 -> x0, waiting for transfers between devices: 197 us -> none  [on_device(): lax.psum_scatter(partial_value, 'layer', scatter_dimension=0, tiled=True)]
    dot_general x8 -> x0, matrix products: 112 us -> none  [one_group(): jnp.einsum('sfij,sfjk->sik', left, right, preferred_element_type=jnp.floa...]
    all_gather x2 -> x0, waiting for transfers between devices: 77 us -> none  [the longest x1 63.8 us: on_device(): gathered_a = lax.all_gather(local_a, 'col', axis=0, tiled=True)]
    pallas_call x0 -> x1, Pallas kernels: none -> 69.6 us  [on_device(): pl.pallas_call(kernel, out_shape=jax.ShapeDtypeStruct((4, TB, TB), jnp.bf...]
  transfers between devices with their start and end apart: 3 -> 0, of which waited for: 3 -> 0; matrix products, arithmetic and copies ran while one was open for 0% -> 0% of each run, Pallas kernels for 0% -> 0%
where the time goes in v2:
time: 73 us; the launch traced here: 72.7 us
  Pallas kernels  69.6 us (95%)
  local copies, waits for them, and re-layouts  2.38 us (3%)
  other arithmetic  0.74 us (1%)
    pallas_call x1, Pallas kernels, on_device(): pl.pallas_call(kernel, out_shape=jax.ShapeDtypeStruct((4, TB, TB), jnp.bf...  69.6 us
    unnamed x1, local copies, waits for them, and re-layouts  1.57 us

profile of v2, /device:TPU:0, one launch (start us, length us, event | category | flops | bytes accessed | tf_op | source)
XLA Modules:
  0.0 72.7 jit_solution(5184509949960265370)
XLA Ops:
  0.0 0.7 %multiply_add_fusion = s32[1,1,1,2,128,16]{4,5,3,2,1,0:T(8,128)S(1)} fusion(s32[1,1,1,2,128,16]{4,5,3,2,1,0:T(8,128)} %param.7, s32[1,1,1,2,128,16]{4,5,3,2,1,0:T(8,128)} %param.6), kind=kLoop, calls=%fused_computation | loop fusion | flops 8192 | bytes 49152 | tf_op jit(solution)/shard_map/add | solution.py:347
  0.7 0.1 copy.6
  0.8 0.7 add.8.pairs
  1.6 69.6 %shard_map.46 = bf16[4,128,128]{2,1,0:T(8,128)(2,1)} custom-call(s32[2,16,128]{2,1,0:T(8,128)} %add.8.pairs, bf16[64,128,128]{2,1,0:T(8,128)(2,1)} %bitcast.6, bf16[16,128,128]{2,1,0:T(8,128)(2,1)} %bitcast.7), custom_call_target="tpu_custom_call" | custom-call | flops 17179869184 | bytes 4194304 | tf_op jit(solution)/shard_map/pallas_call | solution.py:352
  71.2 1.6 %copy.8 = bf16[1,1,4,128,128]{4,3,2,1,0:T(8,128)(2,1)} copy(bf16[1,1,4,128,128]{4,3,2,1,0:T(8,128)(2,1)} %bitcast.5) | data formatting | bytes 262144

commit v3 on v2

--- a/solution.py
+++ b/solution.py
@@ -85,8 +85,8 @@
 
 
 def kernel(
-    pairs, a, p_own, out,
-    p_all, p_land, pair_land, pair_mem, own_sum,
+    pair_a, pair_p, a_own, p_own, out,
+    a, p_all, p_land, pair_land, mem_a, mem_p, own_sum,
     far_out, far_in, near_out, near_in, side_out, side_in, mid_out, mid_in, last_out, last_in,
     local_sem, p_send, p_recv, pair_send, pair_recv,
     far_send, far_recv, near_send, near_recv, side_send, side_recv, mid_send, mid_recv, last_send, last_recv,
@@ -131,10 +131,19 @@
     mine = pl.ds(r * 16, 16)
     theirs = pl.ds((1 - r) * 16, 16)
     own_copy = pltpu.make_async_copy(p_own, p_all.at[mine], local_sem.at[0])
-    pair_copy = pltpu.make_async_copy(pairs.at[q], pair_mem.at[pl.ds(0, 16)], local_sem.at[1])
-    pair_move = pltpu.make_async_copy(pair_land, pair_mem.at[pl.ds(16, 16)], local_sem.at[2])
+    pair_copies = [
+        pltpu.make_async_copy(pair.at[q], mem.at[pl.ds(0, 16)], local_sem.at[1 + i])
+        for i, (pair, mem) in enumerate(((pair_a, mem_a), (pair_p, mem_p)))
+    ]
+    pair_moves = [
+        pltpu.make_async_copy(pair_land.at[i], mem.at[pl.ds(16, 16)], local_sem.at[3 + i])
+        for i, mem in enumerate((mem_a, mem_p))
+    ]
+    a_copy = pltpu.make_async_copy(a_own, a, local_sem.at[5])
     own_copy.start()
-    pair_copy.start()
+    a_copy.start()
+    for copy in pair_copies:
+        copy.start()
     pl.semaphore_wait(barrier, len(others))
 
     def remote(src, dst, send, recv, to):
@@ -144,15 +153,21 @@
         )
 
     to_sibling = remote(p_own, p_all.at[mine], p_send.at[0], p_recv.at[0], sibling)
-    pairs_over = remote(pairs.at[1 - q], pair_land, pair_send, pair_recv, partner)
+    pairs_over = [
+        remote(pair.at[1 - q], pair_land.at[i], pair_send.at[i], pair_recv.at[i], partner)
+        for i, pair in enumerate((pair_a, pair_p))
+    ]
     to_partner = remote(p_own, p_land.at[mine], p_send.at[1], p_recv.at[1], partner)
     forward = remote(p_land.at[mine], p_land.at[mine], p_send.at[2], p_recv.at[2], sibling)
     forward_in = remote(p_land.at[theirs], p_land.at[theirs], p_send.at[2], p_recv.at[2], sibling)
     to_sibling.start()
-    pairs_over.start()
+    for copy in pairs_over:
+        copy.start()
     to_partner.start()
     own_copy.wait()
-    pair_copy.wait()
+    a_copy.wait()
+    for copy in pair_copies:
+        copy.wait()
     to_sibling.wait_recv()
 
     def along(o, d):
@@ -180,15 +195,14 @@
     last = remote(last_out, last_in, last_send, last_recv, across(3))
 
     def product(k, at, o, j):
-        row = (k // 2) * 16 + at
-        lane = turned(x_lo, k % 2) * 64 + o * 32 + j * 16
+        row = (k // 2) * 16
+        lane = at * 8 + turned(x_lo, k % 2) * 4 + o * 2 + j
         first_p = (k // 2) * 32
         total = None
         for g in range(FPC // 2):
-            one = pair_mem[row, lane + 2 * g]
-            two = pair_mem[row, lane + 2 * g + 1]
-            left = jnp.concatenate([a[one >> 5], a[two >> 5]], axis=1)
-            right = jnp.concatenate([p_all[first_p + (one & 31)], p_all[first_p + (two & 31)]], axis=0)
+            one, two = row + 2 * g, row + 2 * g + 1
+            left = jnp.concatenate([a[mem_a[one, lane]], a[mem_a[two, lane]]], axis=1)
+            right = jnp.concatenate([p_all[first_p + mem_p[one, lane]], p_all[first_p + mem_p[two, lane]]], axis=0)
             part = jnp.dot(left, right, preferred_element_type=jnp.float32)
             total = part if total is None else total + part
         return total
@@ -294,11 +308,14 @@
     def take_p():
         to_partner.wait_recv()
         forward.start()
-        pairs_over.wait_recv()
-        pair_move.start()
+        for copy in pairs_over:
+            copy.wait_recv()
+        for copy in pair_moves:
+            copy.start()
 
     def spread_p():
-        pair_move.wait()
+        for copy in pair_moves:
+            copy.wait()
         forward_in.wait_recv()
 
         @pl.loop(0, 32)
@@ -307,9 +324,11 @@
 
     @pl.loop(0, len(ITEMS))
     def _(i):
-        code = 0
-        for n, item in enumerate(ITEMS):
-            code = jnp.where(i == n, ((item[0] * 4 + item[1]) * 2 + item[2]) * 2 + item[3], code)
+        word = 0
+        for n in range(0, len(ITEMS), 4):
+            codes = [((item[0] * 4 + item[1]) * 2 + item[2]) * 2 + item[3] for item in ITEMS[n : n + 4]]
+            word = jnp.where(i // 4 == n // 4, sum(code << (7 * at) for at, code in enumerate(codes)), word)
+        code = (word >> (7 * (i % 4))) & 127
         kind, k, u, d = code // 16, (code // 4) % 4, (code // 2) % 2, code % 2
         pl.when(kind == FAR)(lambda: far_item(k, u))
         pl.when(kind == NEAR)(lambda: near_item(k, u, d))
@@ -326,7 +345,7 @@
     for i in range(4):
         out[i] = (own_sum[4 + i] + decode(last_in, scale, i)).astype(out.dtype)
 
-    for copy in (to_sibling, to_partner, forward, pairs_over, last):
+    for copy in (to_sibling, to_partner, forward, *pairs_over, last):
         copy.wait_send()
 
     @pl.loop(0, 16)
@@ -344,7 +363,7 @@
 
 
 def on_device(a_tiles, p_tiles, pair_a, pair_p):
-    pairs = (pair_a[0, 0, 0] * 32 + pair_p[0, 0, 0]).reshape(2, 16, TB)
+    lists = [jnp.transpose(pair[0, 0, 0], (0, 2, 1)) for pair in (pair_a, pair_p)]
     i16 = jnp.int16
     dma = pltpu.SemaphoreType.DMA
     vmem = pl.BlockSpec(memory_space=pltpu.VMEM)
@@ -352,12 +371,14 @@
     out = pl.pallas_call(
         kernel,
         out_shape=jax.ShapeDtypeStruct((4, TB, TB), jnp.bfloat16),
-        in_specs=[anywhere, vmem, anywhere],
+        in_specs=[anywhere] * 4,
         out_specs=vmem,
         scratch_shapes=[
             pltpu.VMEM((64, TB, TB), jnp.bfloat16),
+            pltpu.VMEM((64, TB, TB), jnp.bfloat16),
             pltpu.VMEM((32, TB, TB), jnp.bfloat16),
-            pltpu.VMEM((16, TB), jnp.int32),
+            pltpu.VMEM((2, 16, TB), jnp.int32),
+            pltpu.SMEM((32, TB), jnp.int32),
             pltpu.SMEM((32, TB), jnp.int32),
             pltpu.VMEM((8, TB, TB), jnp.float32),
             pltpu.VMEM((16, HALF, TB), i16),
@@ -370,7 +391,7 @@
             pltpu.VMEM((12, PAIR, TB), i16),
             pltpu.VMEM((HALF, TB), i16),
             pltpu.VMEM((HALF, TB), i16),
-            dma((3,)), dma((3,)), dma((3,)), dma, dma,
+            dma((6,)), dma((3,)), dma((3,)), dma((2,)), dma((2,)),
             dma((16,)), dma((16,)), dma((16,)), dma((16,)),
             dma((4,)), dma((4,)), dma((12,)), dma((12,)), dma, dma,
         ],
@@ -378,7 +399,7 @@
             collective_id=0, has_side_effects=True, vmem_limit_bytes=56 << 20
         ),
         cost_estimate=pl.CostEstimate(flops=2 * 4096 * TB**3, bytes_accessed=4 << 20, transcendentals=0),
-    )(pairs, a_tiles[0, 0, 0], p_tiles[0, 0, 0])
+    )(*lists, a_tiles[0, 0, 0], p_tiles[0, 0, 0])
     return out[None, None]
 
 

time: 73 us -> 69.2 us (0.948)
  Pallas kernels: 69.6 us -> 67.5 us
  local copies, waits for them, and re-layouts: 2.38 us -> 1.57 us
  other arithmetic: 0.74 us -> 0 us
    pallas_call x1, Pallas kernels: 69.6 us -> 67.5 us  [on_device(): pl.pallas_call(kernel, out_shape=jax.ShapeDtypeStruct((4, TB, TB), jnp.bf...]
    add x2 -> x0, local copies, waits for them, and re-layouts: 0.81 us -> none  [on_device(): pairs = (pair_a[0, 0, 0] * 32 + pair_p[0, 0, 0]).reshape(2, 16, TB)]
    add x1 -> x0, other arithmetic: 0.74 us -> none  [on_device(): pairs = (pair_a[0, 0, 0] * 32 + pair_p[0, 0, 0]).reshape(2, 16, TB)]
where the time goes in v3:
time: 69.2 us; the launch traced here: 69 us
  Pallas kernels  67.5 us (98%)
  local copies, waits for them, and re-layouts  1.57 us (2%)
    pallas_call x1, Pallas kernels, on_device(): pl.pallas_call(kernel, out_shape=jax.ShapeDtypeStruct((4, TB, TB), jnp.bf...  67.5 us
    unnamed x1, local copies, waits for them, and re-layouts  1.57 us

profile of v3, /device:TPU:0, one launch (start us, length us, event | category | flops | bytes accessed | tf_op | source)
XLA Modules:
  0.0 69.0 jit_solution(12365109020652935609)
XLA Ops:
  0.0 67.5 %shard_map.46 = bf16[4,128,128]{2,1,0:T(8,128)(2,1)} custom-call(s32[2,16,128]{2,1,0:T(8,128)} %bitcast.12, s32[2,16,128]{2,1,0:T(8,128)} %bitcast.13, bf16[64,128,128]{2,1,0:T(8,128)(2,1)} %bitcast.10, bf16[16,128,128]{2,1,0:T(8,128)(2,1)} %bitcast.11), custom_call_target="tpu_custom_call" | custom-call | flops 17179869184 | bytes 4194304 | tf_op jit(solution)/shard_map/pallas_call | solution.py:371
  67.5 1.6 %copy.6 = bf16[1,1,4,128,128]{4,3,2,1,0:T(8,128)(2,1)} copy(bf16[1,1,4,128,128]{4,3,2,1,0:T(8,128)(2,1)} %bitcast.9) | data formatting | bytes 262144

commit v4 on v3

--- a/solution.py
+++ b/solution.py
@@ -330,14 +330,17 @@
             word = jnp.where(i // 4 == n // 4, sum(code << (7 * at) for at, code in enumerate(codes)), word)
         code = (word >> (7 * (i % 4))) & 127
         kind, k, u, d = code // 16, (code // 4) % 4, (code // 2) % 2, code % 2
-        pl.when(kind == FAR)(lambda: far_item(k, u))
-        pl.when(kind == NEAR)(lambda: near_item(k, u, d))
-        pl.when(kind == SIDE)(lambda: side_item(k, u))
-        pl.when(kind == MID)(lambda: mid_item(3, 0, u, ()))
-        pl.when(kind == HOME)(lambda: mid_item(0, 1, u, (1, 2)))
-        pl.when(kind == TAKE)(take_p)
-        pl.when(kind == SPREAD)(spread_p)
-        pl.when(kind == OWN)(lambda: own_item(0))
+        pl.when(kind == FAR)(lambda: far_item(k, turned(u, r)))
+        pl.when(kind == NEAR)(lambda: near_item(k, turned(u, r), turned(d, r)))
+
+        @pl.when(kind >= SIDE)
+        def _():
+            pl.when(kind == SIDE)(lambda: side_item(k, u))
+            pl.when(kind == MID)(lambda: mid_item(3, 0, u, ()))
+            pl.when(kind == HOME)(lambda: mid_item(0, 1, u, (1, 2)))
+            pl.when(kind == TAKE)(take_p)
+            pl.when(kind == SPREAD)(spread_p)
+            pl.when(kind == OWN)(lambda: own_item(0))
     own_item(1)
 
     last.wait_recv()

time: 69.2 us -> 67.3 us (0.973)
  Pallas kernels: 67.5 us -> 65.2 us
    pallas_call x1, Pallas kernels: 67.5 us -> 65.2 us  [on_device(): pl.pallas_call(kernel, out_shape=jax.ShapeDtypeStruct((4, TB, TB), jnp.bf...]
where the time goes in v4:
time: 67.3 us; the launch traced here: 66.7 us
  Pallas kernels  65.2 us (97%)
  local copies, waits for them, and re-layouts  1.57 us (2%)
    pallas_call x1, Pallas kernels, on_device(): pl.pallas_call(kernel, out_shape=jax.ShapeDtypeStruct((4, TB, TB), jnp.bf...  65.2 us
    unnamed x1, local copies, waits for them, and re-layouts  1.57 us

profile of v4, /device:TPU:0, one launch (start us, length us, event | category | flops | bytes accessed | tf_op | source)
XLA Modules:
  0.0 66.7 jit_solution(5129670844180361702)
XLA Ops:
  0.0 65.2 %shard_map.46 = bf16[4,128,128]{2,1,0:T(8,128)(2,1)} custom-call(s32[2,16,128]{2,1,0:T(8,128)} %bitcast.12, s32[2,16,128]{2,1,0:T(8,128)} %bitcast.13, bf16[64,128,128]{2,1,0:T(8,128)(2,1)} %bitcast.10, bf16[16,128,128]{2,1,0:T(8,128)(2,1)} %bitcast.11), custom_call_target="tpu_custom_call" | custom-call | flops 17179869184 | bytes 4194304 | tf_op jit(solution)/shard_map/pallas_call | solution.py:374
  65.2 1.6 %copy.6 = bf16[1,1,4,128,128]{4,3,2,1,0:T(8,128)(2,1)} copy(bf16[1,1,4,128,128]{4,3,2,1,0:T(8,128)(2,1)} %bitcast.9) | data formatting | bytes 262144

commit v5 on v4

--- a/solution.py
+++ b/solution.py
@@ -216,6 +216,7 @@
                 sums[j].append(product(k, at, o, j))
         for d in range(2):
             encode(sums[d], far_out.at[(k * 2 + o) * 2 + d])
+        for d in range(2):
             far(k, o, d).start()
 
     def near_item(k, o, d):
@@ -268,22 +269,19 @@
 
     def mid_item(k, h, g, extra):
         sums = mid_sums(k, g, extra)
+        kk = 2 - g
         for o in range(2):
-            kk = 2 - g
             encode(sums[o * 4 : o * 4 + 2], mid_out.at[(h * 2 + o) * 3 + kk - 1])
+            encode(sums[o * 4 + 2 : o * 4 + 4], mid_out.at[((h * 2 + o) * 3 + 2) * (1 - g) + 12 * g])
+            for j in range(2):
+                own_sum[h * 4 + o * 2 + j] = sums[o * 4 + 2 + j]
+        for o in range(2):
             mid(h, o, kk).start()
 
         @pl.when(g == 0)
         def _():
             for o in range(2):
-                encode(sums[o * 4 + 2 : o * 4 + 4], mid_out.at[(h * 2 + o) * 3 + 2])
                 mid(h, o, 3).start()
-
-        @pl.when(g == 1)
-        def _():
-            for o in range(2):
-                for j in range(2):
-                    own_sum[h * 4 + o * 2 + j] = sums[o * 4 + 2 + j]
 
     def own_item(h):
         sums = []
@@ -390,7 +388,7 @@
             pltpu.VMEM((16, FULL, TB), i16),
             pltpu.VMEM((4, FULL, TB), i16),
             pltpu.VMEM((4, FULL, TB), i16),
-            pltpu.VMEM((12, PAIR, TB), i16),
+            pltpu.VMEM((13, PAIR, TB), i16),
             pltpu.VMEM((12, PAIR, TB), i16),
             pltpu.VMEM((HALF, TB), i16),
             pltpu.VMEM((HALF, TB), i16),

time: 67.3 us -> 67.6 us (level)
  no operation moved by 1% of the time
where the time goes in v5:
time: 67.6 us; the launch traced here: 67 us
  Pallas kernels  65.4 us (97%)
  local copies, waits for them, and re-layouts  1.57 us (2%)
    pallas_call x1, Pallas kernels, on_device(): pl.pallas_call(kernel, out_shape=jax.ShapeDtypeStruct((4, TB, TB), jnp.bf...  65.4 us
    unnamed x1, local copies, waits for them, and re-layouts  1.57 us

profile of v5, /device:TPU:0, one launch (start us, length us, event | category | flops | bytes accessed | tf_op | source)
XLA Modules:
  0.0 67.0 jit_solution(1958822772545780818)
XLA Ops:
  0.0 65.4 %shard_map.46 = bf16[4,128,128]{2,1,0:T(8,128)(2,1)} custom-call(s32[2,16,128]{2,1,0:T(8,128)} %bitcast.12, s32[2,16,128]{2,1,0:T(8,128)} %bitcast.13, bf16[64,128,128]{2,1,0:T(8,128)(2,1)} %bitcast.10, bf16[16,128,128]{2,1,0:T(8,128)(2,1)} %bitcast.11), custom_call_target="tpu_custom_call" | custom-call | flops 17179869184 | bytes 4194304 | tf_op jit(solution)/shard_map/pallas_call | solution.py:372
  65.4 1.6 %copy.6 = bf16[1,1,4,128,128]{4,3,2,1,0:T(8,128)(2,1)} copy(bf16[1,1,4,128,128]{4,3,2,1,0:T(8,128)(2,1)} %bitcast.9) | data formatting | bytes 262144

commit v6 on v5

--- a/solution.py
+++ b/solution.py
@@ -276,12 +276,12 @@
             for j in range(2):
                 own_sum[h * 4 + o * 2 + j] = sums[o * 4 + 2 + j]
         for o in range(2):
-            mid(h, o, kk).start()
+            mid(h, turned(o, r), kk).start()
 
         @pl.when(g == 0)
         def _():
             for o in range(2):
-                mid(h, o, 3).start()
+                mid(h, turned(o, r), 3).start()
 
     def own_item(h):
         sums = []

time: 67.6 us -> 67.6 us (level)
  no operation moved by 1% of the time
where the time goes in v6:
time: 67.6 us; the launch traced here: 67 us
  Pallas kernels  65.4 us (97%)
  local copies, waits for them, and re-layouts  1.57 us (2%)
    pallas_call x1, Pallas kernels, on_device(): pl.pallas_call(kernel, out_shape=jax.ShapeDtypeStruct((4, TB, TB), jnp.bf...  65.4 us
    unnamed x1, local copies, waits for them, and re-layouts  1.57 us

profile of v6, /device:TPU:0, one launch (start us, length us, event | category | flops | bytes accessed | tf_op | source)
XLA Modules:
  0.0 67.0 jit_solution(17932540993299794427)
XLA Ops:
  0.0 65.4 %shard_map.46 = bf16[4,128,128]{2,1,0:T(8,128)(2,1)} custom-call(s32[2,16,128]{2,1,0:T(8,128)} %bitcast.12, s32[2,16,128]{2,1,0:T(8,128)} %bitcast.13, bf16[64,128,128]{2,1,0:T(8,128)(2,1)} %bitcast.10, bf16[16,128,128]{2,1,0:T(8,128)(2,1)} %bitcast.11), custom_call_target="tpu_custom_call" | custom-call | flops 17179869184 | bytes 4194304 | tf_op jit(solution)/shard_map/pallas_call | solution.py:372
  65.4 1.6 %copy.6 = bf16[1,1,4,128,128]{4,3,2,1,0:T(8,128)(2,1)} copy(bf16[1,1,4,128,128]{4,3,2,1,0:T(8,128)(2,1)} %bitcast.9) | data formatting | bytes 262144
